TPU v7x, 32 devices: a whole 2x2x4 slice. The times are simulated.
32 devices in a mesh: dp: 2 (over core), region: 16 (over z, y, x).
Axes of the slice: x: 2, y: 2, z: 4, core: 2. Of those that a mesh axis runs over, the one named last changes fastest.
Arguments:
- cell_counts: int32 [16384], P('dp'), may hold values from 61 to 6144, as said below
- cell_seeds: int32 [16384], P('dp'), may hold values from 0 to 12287
- batch_ids: int32 [16384], P('dp'), may hold values from 0 to 7
- noise_draw: float32 [16384, 10], P('dp'), may hold values from -4 to 4
- cell_factor: float32 [16384], P('dp'), may hold values from 0.3 to 0.95
- enc_weight: float32 [12288, 128], P('region', 'dp'), may hold values from -0.0546875 to 0.0546875
- enc_first: float32 [12288, 128], P('region', 'dp'), may hold values from -1.1444092e-05 to 1.1444092e-05
- enc_second: float32 [12288, 128], P('region', 'dp'), may hold values from 3.4924596e-12 to 1.3969838e-11
- dec_weight: float32 [128, 12288], P('dp', 'region'), may hold values from -0.5 to 0.5
- dec_first: float32 [128, 12288], P('dp', 'region'), may hold values from -7.1525574e-07 to 7.1525574e-07
- dec_second: float32 [128, 12288], P('dp', 'region'), may hold values from 1.6168795e-14 to 6.467518e-14
- region_vecs: float32 [2, 12288], P('dp', 'region')
- vec_first: float32 [2, 12288], P('dp', 'region'), may hold values from -1.335144e-05 to 1.335144e-05
- vec_second: float32 [2, 12288], P('dp', 'region'), may hold values from 4.6566128e-12 to 1.8626451e-11
- trunk_rows: float32 [290, 128], replicated
- trunk_first: float32 [290, 128], replicated, may hold values from -1.5258789e-05 to 1.5258789e-05
- trunk_second: float32 [290, 128], replicated, may hold values from 6.2088173e-12 to 2.483527e-11
- head_rows: float32 [129, 20], replicated
- head_first: float32 [129, 20], replicated, may hold values from -1.5258789e-05 to 1.5258789e-05
- head_second: float32 [129, 20], replicated, may hold values from 6.2088173e-12 to 2.483527e-11
Outputs:
- loss: float32 [2], replicated
- enc_new: float32 [12288, 128], P('region', 'dp')
- enc_first_new: float32 [12288, 128], P('region', 'dp')
- enc_second_new: float32 [12288, 128], P('region', 'dp')
- enc_copy: bfloat16 [12288, 128], P('region', 'dp')
- dec_new: float32 [128, 12288], P('dp', 'region')
- dec_first_new: float32 [128, 12288], P('dp', 'region')
- dec_second_new: float32 [128, 12288], P('dp', 'region')
- dec_copy: bfloat16 [128, 12288], P('dp', 'region')
- vecs_new: float32 [2, 12288], P('dp', 'region')
- vec_first_new: float32 [2, 12288], P('dp', 'region')
- vec_second_new: float32 [2, 12288], P('dp', 'region')
- trunk_new: float32 [290, 128], replicated
- trunk_first_new: float32 [290, 128], replicated
- trunk_second_new: float32 [290, 128], replicated
- head_new: float32 [129, 20], replicated
- head_first_new: float32 [129, 20], replicated
- head_second_new: float32 [129, 20], replicated
- norms: float32 [2, 10], replicated
Inputs may be any that keep to these rules, and one draw needn't show every extreme that they name: Each cell opens exactly cell_counts regions, given by the rule of the first step; some cell holds the smallest and some the largest count.
All inputs are finite; a program needn't handle non-finite values.
Results may differ from a plain program's by a relative error of at most 0.002.
The roundings to bfloat16 on the way count: a program that leaves them out, or rounds other values in their place, can miss the bound.
Values may be sent and summed in bfloat16 or wider, within the bound.
No kernel may reach another device: no remote copies, remote signals or barrier semaphores. Data moves between devices by JAX's collectives and lax.ppermute only.
A program may use at most 128 MiB of HBM per device.

v0:
```python
import jax
import jax.numpy as jnp
from jax import lax
from jax.sharding import PartitionSpec as P

BATCHES = 8
highest = lax.Precision.HIGHEST
norm_eps = 1e-05
leak_slope = 0.01
decay_rate = 0.5
weight_decay = 0.01
learn_rate = 0.5
lamb_eps = 1e-12


def matmul(left, right):
    return jnp.dot(left, right, precision=highest, preferred_element_type=jnp.float32)


def layer_norm(values, gain_row, shift_row):
    centre = values - jnp.mean(values, axis=-1, keepdims=True)
    spread = jnp.mean(centre * centre, axis=-1, keepdims=True)
    return centre * lax.rsqrt(spread + norm_eps) * gain_row + shift_row


def leaky_relu(values):
    return jnp.where(values >= 0, values, leak_slope * values)


def region_masks(counts, seed_rows, first_region, width, total):
    regions = first_region + jnp.arange(width, dtype=jnp.int32)
    stride = 6 * (seed_rows % (total // 6)) + 1
    upper = stride[:, None] * (regions[None, :] // 256) % total
    hashed = (upper * 256 + stride[:, None] * (regions[None, :] % 256) + seed_rows[:, None]) % total
    return hashed < counts[:, None]


def trunk_forward(pre_in, trunk_part, head_part, noise_rows, onehot):
    hidden = trunk_part.shape[1]
    latent = head_part.shape[1] // 2
    batches = onehot.shape[1]
    enc_two = trunk_part[batches : batches + hidden]
    dec_one = trunk_part[batches + hidden : 2 * batches + hidden + latent]
    dec_two = trunk_part[2 * batches + hidden + latent : 2 * batches + 2 * hidden + latent]
    base_row = 2 * batches + 2 * hidden + latent
    gain_rows = trunk_part[base_row : base_row + 4]
    shift_rows = trunk_part[base_row + 4 : base_row + 8]
    first = leaky_relu(layer_norm(pre_in, gain_rows[0], shift_rows[0]))
    second = leaky_relu(layer_norm(matmul(first, enc_two), gain_rows[1], shift_rows[1]))
    moments = matmul(second, head_part[:hidden]) + head_part[hidden]
    centre_lat = moments[:, :latent]
    log_var = moments[:, latent:]
    sample = centre_lat + jnp.exp(0.5 * log_var) * noise_rows
    third_in = matmul(sample, dec_one[:latent]) + matmul(onehot, dec_one[latent:])
    third = leaky_relu(layer_norm(third_in, gain_rows[2], shift_rows[2]))
    fourth = leaky_relu(layer_norm(matmul(third, dec_two), gain_rows[3], shift_rows[3]))
    diverge = 0.5 * jnp.sum(jnp.exp(log_var) + centre_lat * centre_lat - 1.0 - log_var)
    return (fourth, diverge)


def lamb_moments(weight, grad, first, second):
    first_new = decay_rate * first + (1.0 - decay_rate) * grad
    second_new = decay_rate * second + (1.0 - decay_rate) * grad * grad
    update = first_new / (jnp.sqrt(second_new) + lamb_eps) + weight_decay * weight
    return (first_new, second_new, update)


def square_norm(values):
    return jnp.sqrt(jnp.sum(values * values))


def lamb_groups(weight, update, row_edges):
    pieces = []
    weight_list = []
    update_list = []
    for group_index in range(len(row_edges) - 1):
        start_row = row_edges[group_index]
        end_row = row_edges[group_index + 1]
        weight_part = weight[start_row:end_row]
        update_part = update[start_row:end_row]
        weight_norm = square_norm(weight_part)
        update_norm = square_norm(update_part)
        weight_list.append(weight_norm)
        update_list.append(update_norm)
        pieces.append(weight_part - learn_rate * (weight_norm / update_norm) * update_part)
    return (jnp.concatenate(pieces, axis=0), jnp.stack(weight_list), jnp.stack(update_list))


def weight_squares(enc_weight, dec_weight, region_vecs, slot_rows):
    pair = jnp.stack([jnp.sum(enc_weight * enc_weight), jnp.sum(dec_weight * dec_weight)])
    return jnp.concatenate([pair, slot_rows * jnp.sum(region_vecs * region_vecs)])


def on_device(
    cell_counts,
    cell_seeds,
    batch_ids,
    noise_draw,
    cell_factor,
    enc_weight,
    enc_first,
    enc_second,
    dec_weight,
    dec_first,
    dec_second,
    region_vecs,
    vec_first,
    vec_second,
    trunk_rows,
    trunk_first,
    trunk_second,
    head_rows,
    head_first,
    head_second,
):
    cells_here = cell_counts.shape[0]
    regions_here = enc_weight.shape[0]
    hidden = trunk_rows.shape[1]
    latent = head_rows.shape[1] // 2
    region_count = lax.axis_size("region")
    total_regions = regions_here * region_count
    all_cells = cells_here * lax.axis_size("dp")
    loss_scale = 1.0 / (all_cells * total_regions)
    first_region = lax.axis_index("region") * regions_here
    row_index = lax.axis_index("dp")
    slot_rows = (jnp.arange(2, dtype=jnp.int32) == row_index).astype(jnp.float32)
    block_rows = min(1024, cells_here)
    blocks = cells_here // block_rows
    enc_low, dec_low, vec_low = (
        lax.all_gather(enc_weight.astype(jnp.bfloat16), "dp", axis=1, tiled=True),
        lax.all_gather(dec_weight.astype(jnp.bfloat16), "dp", axis=0, tiled=True),
        lax.all_gather(region_vecs.astype(jnp.bfloat16), "dp", axis=0, tiled=True),
    )
    counts_blocks = cell_counts.reshape(blocks, block_rows)
    seed_blocks = cell_seeds.reshape(blocks, block_rows)

    def encode_block(carried, inputs):
        mask_rows = region_masks(
            inputs[0], inputs[1], first_region, regions_here, total_regions
        ).astype(jnp.bfloat16)
        return (carried, jnp.dot(mask_rows, enc_low, preferred_element_type=jnp.float32))

    _, partial_pre = lax.scan(
        encode_block, jnp.zeros((), jnp.float32), (counts_blocks, seed_blocks)
    )
    partial_pre = partial_pre.reshape(cells_here, hidden)
    onehot = (batch_ids[:, None] == jnp.arange(BATCHES, dtype=jnp.int32)[None, :]).astype(
        jnp.float32
    )
    onehot_low = onehot.astype(jnp.bfloat16)
    enc_total = lax.psum(partial_pre, "region")
    pre_one = enc_total + matmul(onehot, trunk_rows[:BATCHES])
    (decoded, diverge), pull_back = jax.vjp(
        lambda pre_in, weights, head_part: trunk_forward(
            pre_in, weights, head_part, noise_draw, onehot
        ),
        pre_one,
        trunk_rows,
        head_rows,
    )
    decoded_low = decoded.astype(jnp.bfloat16)
    decoded_blocks = decoded_low.reshape(blocks, block_rows, hidden)
    factor_blocks = cell_factor.reshape(blocks, block_rows)
    region_bias = vec_low[0].astype(jnp.float32)
    region_logit = vec_low[1].astype(jnp.float32)
    log_region = jax.nn.log_sigmoid(region_logit)
    keep_region = jax.nn.sigmoid(-region_logit)

    def decode_block(carried, inputs):
        grad_dec, grad_bias, grad_logit, recon_sum = carried
        counts, seed_rows, hidden_low, factors = inputs
        mask_rows = region_masks(
            counts, seed_rows, first_region, regions_here, total_regions
        ).astype(jnp.float32)
        logits = jnp.dot(hidden_low, dec_low, preferred_element_type=jnp.float32) + region_bias
        log_prob = jax.nn.log_sigmoid(logits) + jnp.log(factors)[:, None] + log_region[None, :]
        probability = jnp.exp(log_prob)
        recon_sum = recon_sum - jnp.sum(
            mask_rows * log_prob + (1.0 - mask_rows) * jnp.log1p(-probability)
        )
        signal = (mask_rows - (1.0 - mask_rows) * probability / (1.0 - probability)) * loss_scale
        grad_logits = (-jax.nn.sigmoid(-logits) * signal).astype(jnp.bfloat16)
        grad_dec = grad_dec + lax.dot_general(
            hidden_low, grad_logits, (((0,), (0,)), ((), ())), preferred_element_type=jnp.float32
        )
        grad_bias = grad_bias + jnp.sum(grad_logits, axis=0, dtype=jnp.float32)
        grad_logit = grad_logit - keep_region * jnp.sum(signal, axis=0)
        back_part = lax.dot_general(
            grad_logits, dec_low, (((1,), (1,)), ((), ())), preferred_element_type=jnp.float32
        )
        return ((grad_dec, grad_bias, grad_logit, recon_sum), back_part)

    initial = (
        jnp.zeros((hidden, regions_here), jnp.float32),
        jnp.zeros((regions_here,), jnp.float32),
        jnp.zeros((regions_here,), jnp.float32),
        jnp.zeros((), jnp.float32),
    )
    (grad_dec, grad_bias, grad_logit, recon_sum), back_parts = lax.scan(
        decode_block, initial, (counts_blocks, seed_blocks, decoded_blocks, factor_blocks)
    )
    back_hidden = back_parts.reshape(cells_here, hidden)
    hidden_grad, recon_region = lax.psum((back_hidden, recon_sum), "region")
    grad_pre, grad_trunk, grad_head = pull_back((hidden_grad, jnp.float32(loss_scale)))
    pre_low = grad_pre.astype(jnp.bfloat16)
    batch_grad = lax.dot_general(
        onehot_low, pre_low, (((0,), (0,)), ((), ())), preferred_element_type=jnp.float32
    )
    grad_trunk = grad_trunk.at[:BATCHES].add(batch_grad)
    grad_trunk, grad_head, recon_all, diverge_all = lax.psum(
        (grad_trunk, grad_head, recon_region, diverge), "dp"
    )
    pre_blocks = pre_low.reshape(blocks, block_rows, hidden)

    def encode_back(carried, inputs):
        mask_rows = region_masks(
            inputs[0], inputs[1], first_region, regions_here, total_regions
        ).astype(jnp.bfloat16)
        return (
            carried
            + lax.dot_general(
                mask_rows, inputs[2], (((0,), (0,)), ((), ())), preferred_element_type=jnp.float32
            ),
            None,
        )

    grad_enc, _ = lax.scan(
        encode_back,
        jnp.zeros((regions_here, hidden), jnp.float32),
        (counts_blocks, seed_blocks, pre_blocks),
    )
    grad_vecs = jnp.stack([grad_bias, grad_logit])
    grad_enc, grad_dec, grad_vecs = (
        lax.psum_scatter(grad_enc, "dp", scatter_dimension=1, tiled=True),
        lax.psum_scatter(grad_dec, "dp", scatter_dimension=0, tiled=True),
        lax.psum_scatter(grad_vecs, "dp", scatter_dimension=0, tiled=True),
    )
    enc_first_new, enc_second_new, enc_update = lamb_moments(
        enc_weight, grad_enc, enc_first, enc_second
    )
    dec_first_new, dec_second_new, dec_update = lamb_moments(
        dec_weight, grad_dec, dec_first, dec_second
    )
    vec_first_new, vec_second_new, vec_update = lamb_moments(
        region_vecs, grad_vecs, vec_first, vec_second
    )
    update_local = weight_squares(enc_update, dec_update, vec_update, slot_rows)
    weight_sums, update_sums = lax.psum(
        (weight_squares(enc_weight, dec_weight, region_vecs, slot_rows), update_local),
        ("dp", "region"),
    )
    region_wn = jnp.sqrt(weight_sums)
    region_un = jnp.sqrt(update_sums)
    enc_new = enc_weight - learn_rate * (region_wn[0] / region_un[0]) * enc_update
    dec_new = dec_weight - learn_rate * (region_wn[1] / region_un[1]) * dec_update
    vec_ratio = jnp.where(row_index == 0, region_wn[2] / region_un[2], region_wn[3] / region_un[3])
    vecs_new = region_vecs - learn_rate * vec_ratio * vec_update
    trunk_first_new, trunk_second_new, trunk_update = lamb_moments(
        trunk_rows, grad_trunk, trunk_first, trunk_second
    )
    head_first_new, head_second_new, head_update = lamb_moments(
        head_rows, grad_head, head_first, head_second
    )
    row_edges = [
        0,
        BATCHES,
        BATCHES + hidden,
        2 * BATCHES + hidden + latent,
        2 * BATCHES + 2 * hidden + latent,
        2 * BATCHES + 2 * hidden + latent + 8,
    ]
    trunk_new, trunk_wn, trunk_un = lamb_groups(trunk_rows, trunk_update, row_edges)
    head_new, head_wn, head_un = lamb_groups(head_rows, head_update, [0, hidden + 1])
    norms = jnp.stack(
        [
            jnp.concatenate([region_wn, trunk_wn, head_wn]),
            jnp.concatenate([region_un, trunk_un, head_un]),
        ]
    )
    loss = jnp.stack([recon_all * loss_scale, diverge_all / all_cells])
    return (
        loss,
        enc_new,
        enc_first_new,
        enc_second_new,
        enc_new.astype(jnp.bfloat16),
        dec_new,
        dec_first_new,
        dec_second_new,
        dec_new.astype(jnp.bfloat16),
        vecs_new,
        vec_first_new,
        vec_second_new,
        trunk_new,
        trunk_first_new,
        trunk_second_new,
        head_new,
        head_first_new,
        head_second_new,
        norms,
    )


def solution(mesh):
    return jax.shard_map(
        on_device,
        mesh=mesh,
        in_specs=(
            P("dp"),
            P("dp"),
            P("dp"),
            P("dp", None),
            P("dp"),
            P("region", "dp"),
            P("region", "dp"),
            P("region", "dp"),
            P("dp", "region"),
            P("dp", "region"),
            P("dp", "region"),
            P("dp", "region"),
            P("dp", "region"),
            P("dp", "region"),
            P(),
            P(),
            P(),
            P(),
            P(),
            P(),
        ),
        out_specs=(
            P(),
            P("region", "dp"),
            P("region", "dp"),
            P("region", "dp"),
            P("region", "dp"),
            P("dp", "region"),
            P("dp", "region"),
            P("dp", "region"),
            P("dp", "region"),
            P("dp", "region"),
            P("dp", "region"),
            P("dp", "region"),
            P(),
            P(),
            P(),
            P(),
            P(),
            P(),
            P(),
        ),
        check_vma=False,
    )
```

profile of v0, /device:TPU:0, one launch (start us, length us, event | category | flops | bytes accessed | tf_op | source)
XLA Modules:
  0.0 877.8 jit_solution(4330750522462627467)
XLA Ops:
  15.5 51.1 %while.50 = (s32[]{:T(128)}, f32[8,1024,128]{2,1,0:T(8,128)}, s32[8,1024]{1,0:T(8,128)}, s32[]{:T(128)}, s32[8,1024]{1,0:T(8,128)}, /*index=5*/bf16[768,128]{1,0:T(8,128)(2,1)S(1)}, s32[]{:T(128)}) while((s32[]{:T(128)}, f32[8,1024,128]{2,1,0:T(8,128)}, s32[8,1024]{1,0:T(8,128)}, s32[]{:T(128)}, s32[8,1024]{1,0:T(8,128)}, ...), condition=%wide.region_1.2_spmd, body=%wide.region_0.1_spmd.sunk | while | flops 215511040 | bytes 770645 | solution.py:143
  72.8 164.7 %all-reduce.26.cloned.1.call-done = f32[8192,128]{1,0:T(8,128)} async-done(((f32[8192,128]{1,0:T(8,128)}), f32[8192,128]{1,0:T(8,128)}) %all-reduce.26.cloned.1.call-update) | async-done | bytes 4194320 | tf_op jit(solution)/shard_map/psum | solution.py:151
  237.6 6.2 fusion.224
  246.2 8.2 fusion.225
  269.9 6.7 fusion.188
  299.3 146.1 %while.51 = (s32[]{:T(128)}, f32[128,768]{1,0:T(8,128)S(1)}, f32[768]{0:T(1024)S(1)}, f32[768]{0:T(1024)}, f32[]{:T(128)}, /*index=5*/f32[8,1024,128]{2,1,0:T(8,...) while((s32[]{:T(128)}, f32[128,768]{1,0:T(8,128)S(1)}, ...), condition=%wide.region_15.16_spmd.clone, body=%wide.region_11.15_spmd.clone.sunk | while | flops 643528960 | bytes 19630788 | solution.py:199
  301.1 10.9 %fusion.260 = (f32[768]{0:T(1024)}, f32[1024,768]{1,0:T(8,128)S(1)}, f32[]{:T(128)}, f32[1024,768]{1,0:T(8,128)S(1)}) fusion(f32[768]{0:T(1024)} %get-tuple-element.1021, f32[1024]{0:T(1024)S(1)} %bitcast.133, f32[768]{0:T(1024)S(1)} %get-tuple-element.1016, s32[1024]{0:T(1024)S(1)} %bitcast.134, s32[1024]{0:T(1024)S(1)} %bitcast.128, ...), kind=kOutput, calls=%fused_computation.378.clone.1 | convolution fusion | flops 234355968 | bytes 6783492 | tf_op jit(solution)/shard_map/while/body/eval_jaxpr/dot_general | solution.py:175
  319.3 10.9 %fusion.260 = (f32[768]{0:T(1024)}, f32[1024,768]{1,0:T(8,128)S(1)}, f32[]{:T(128)}, f32[1024,768]{1,0:T(8,128)S(1)}) fusion(f32[768]{0:T(1024)} %get-tuple-element.1021, f32[1024]{0:T(1024)S(1)} %bitcast.133, f32[768]{0:T(1024)S(1)} %get-tuple-element.1016, s32[1024]{0:T(1024)S(1)} %bitcast.134, s32[1024]{0:T(1024)S(1)} %bitcast.128, ...), kind=kOutput, calls=%fused_computation.378.clone.1 | convolution fusion | flops 234355968 | bytes 6783492 | tf_op jit(solution)/shard_map/while/body/eval_jaxpr/dot_general | solution.py:175
  337.5 10.9 %fusion.260 = (f32[768]{0:T(1024)}, f32[1024,768]{1,0:T(8,128)S(1)}, f32[]{:T(128)}, f32[1024,768]{1,0:T(8,128)S(1)}) fusion(f32[768]{0:T(1024)} %get-tuple-element.1021, f32[1024]{0:T(1024)S(1)} %bitcast.133, f32[768]{0:T(1024)S(1)} %get-tuple-element.1016, s32[1024]{0:T(1024)S(1)} %bitcast.134, s32[1024]{0:T(1024)S(1)} %bitcast.128, ...), kind=kOutput, calls=%fused_computation.378.clone.1 | convolution fusion | flops 234355968 | bytes 6783492 | tf_op jit(solution)/shard_map/while/body/eval_jaxpr/dot_general | solution.py:175
  355.8 10.9 %fusion.260 = (f32[768]{0:T(1024)}, f32[1024,768]{1,0:T(8,128)S(1)}, f32[]{:T(128)}, f32[1024,768]{1,0:T(8,128)S(1)}) fusion(f32[768]{0:T(1024)} %get-tuple-element.1021, f32[1024]{0:T(1024)S(1)} %bitcast.133, f32[768]{0:T(1024)S(1)} %get-tuple-element.1016, s32[1024]{0:T(1024)S(1)} %bitcast.134, s32[1024]{0:T(1024)S(1)} %bitcast.128, ...), kind=kOutput, calls=%fused_computation.378.clone.1 | convolution fusion | flops 234355968 | bytes 6783492 | tf_op jit(solution)/shard_map/while/body/eval_jaxpr/dot_general | solution.py:175
  374.0 10.9 %fusion.260 = (f32[768]{0:T(1024)}, f32[1024,768]{1,0:T(8,128)S(1)}, f32[]{:T(128)}, f32[1024,768]{1,0:T(8,128)S(1)}) fusion(f32[768]{0:T(1024)} %get-tuple-element.1021, f32[1024]{0:T(1024)S(1)} %bitcast.133, f32[768]{0:T(1024)S(1)} %get-tuple-element.1016, s32[1024]{0:T(1024)S(1)} %bitcast.134, s32[1024]{0:T(1024)S(1)} %bitcast.128, ...), kind=kOutput, calls=%fused_computation.378.clone.1 | convolution fusion | flops 234355968 | bytes 6783492 | tf_op jit(solution)/shard_map/while/body/eval_jaxpr/dot_general | solution.py:175
  392.3 10.9 %fusion.260 = (f32[768]{0:T(1024)}, f32[1024,768]{1,0:T(8,128)S(1)}, f32[]{:T(128)}, f32[1024,768]{1,0:T(8,128)S(1)}) fusion(f32[768]{0:T(1024)} %get-tuple-element.1021, f32[1024]{0:T(1024)S(1)} %bitcast.133, f32[768]{0:T(1024)S(1)} %get-tuple-element.1016, s32[1024]{0:T(1024)S(1)} %bitcast.134, s32[1024]{0:T(1024)S(1)} %bitcast.128, ...), kind=kOutput, calls=%fused_computation.378.clone.1 | convolution fusion | flops 234355968 | bytes 6783492 | tf_op jit(solution)/shard_map/while/body/eval_jaxpr/dot_general | solution.py:175
  410.5 10.9 %fusion.260 = (f32[768]{0:T(1024)}, f32[1024,768]{1,0:T(8,128)S(1)}, f32[]{:T(128)}, f32[1024,768]{1,0:T(8,128)S(1)}) fusion(f32[768]{0:T(1024)} %get-tuple-element.1021, f32[1024]{0:T(1024)S(1)} %bitcast.133, f32[768]{0:T(1024)S(1)} %get-tuple-element.1016, s32[1024]{0:T(1024)S(1)} %bitcast.134, s32[1024]{0:T(1024)S(1)} %bitcast.128, ...), kind=kOutput, calls=%fused_computation.378.clone.1 | convolution fusion | flops 234355968 | bytes 6783492 | tf_op jit(solution)/shard_map/while/body/eval_jaxpr/dot_general | solution.py:175
  428.7 10.9 %fusion.260 = (f32[768]{0:T(1024)}, f32[1024,768]{1,0:T(8,128)S(1)}, f32[]{:T(128)}, f32[1024,768]{1,0:T(8,128)S(1)}) fusion(f32[768]{0:T(1024)} %get-tuple-element.1021, f32[1024]{0:T(1024)S(1)} %bitcast.133, f32[768]{0:T(1024)S(1)} %get-tuple-element.1016, s32[1024]{0:T(1024)S(1)} %bitcast.134, s32[1024]{0:T(1024)S(1)} %bitcast.128, ...), kind=kOutput, calls=%fused_computation.378.clone.1 | convolution fusion | flops 234355968 | bytes 6783492 | tf_op jit(solution)/shard_map/while/body/eval_jaxpr/dot_general | solution.py:175
  452.9 43.1 %psum.64 = f32[]{:T(128)} all-reduce(f32[]{:T(128)} %get-tuple-element.495), channel_id=1, replica_groups=mesh['dp'=2,'region'=16] {'region'}, use_global_device_ids=true, to_apply=%region_16.17 | all-reduce | flops 1 | bytes 8 | tf_op jit(solution)/shard_map/psum | solution.py:203
  498.5 130.4 %all-reduce.28.cloned.1.call-done = f32[8192,128]{1,0:T(8,128)} async-done(((f32[8192,128]{1,0:T(8,128)}), f32[8192,128]{1,0:T(8,128)}) %all-reduce.28.cloned.1.call-update) | async-done | bytes 4194320 | tf_op jit(solution)/shard_map/psum | solution.py:203
  628.9 7.6 fusion.208
  641.8 6.4 multiply_reduce_fusion.2
  662.8 11.2 %multiply_reduce_fusion.1 = (f32[128]{0:T(128)}, f32[8192]{0:T(1024)S(1)}, f32[128]{0:T(128)}, f32[8192,128]{1,0:T(8,128)S(1)}) fusion(f32[8192,128]{1,0:T(8,128)S(1)} %copy-done.3, f32[8192]{0:T(1024)S(1)} %copy-done.50, f32[8192]{0:T(1024)S(1)} %copy-done.29, f32[128]{0:T(128)S(1)} %copy-done.67, f32[129,20]{0,1:T(8,128)S(1)} %copy-done.44, ...), kind=kOutput, calls=%fused_computation.162 | convolution fusion | flops 267542272 | bytes 9549824 | tf_op jit(solution)/shard_map/transpose(jvp())/dot_general | solution.py:17
  673.9 11.3 %fusion.109 = f32[128,128]{1,0:T(8,128)} fusion(f32[8192,128]{1,0:T(8,128)S(1)} %get-tuple-element.698, f32[8192,128]{1,0:T(8,128)S(1)} %copy-done.7, f32[8192]{0:T(1024)S(1)} %negate_multiply_fusion.3, f32[128]{0:T(128)S(1)} %copy-done.75, f32[128]{0:T(128)S(1)} %copy-done.69, f32[8192]{0:T(1024)S(1)} %copy-done.52, f32[8192]{0:T(1024)S(1)} %copy-done.31), kind=kOutput, calls=%fused_computation.186 | convolution fusion | flops 1619001344 | bytes 8553472 | tf_op jit(solution)/shard_map/transpose(jvp())/dot_general | solution.py:17
  695.7 8.0 multiply_reduce_fusion
  703.7 10.9 %fusion.103 = f32[128,128]{1,0:T(8,128)} fusion(f32[8192,128]{1,0:T(8,128)S(1)} %get-tuple-element.692, f32[8192,128]{1,0:T(8,128)S(1)} %copy-done.5, f32[8192]{0:T(1024)S(1)} %negate_multiply_fusion.1, f32[128]{0:T(128)S(1)} %copy-done.73, f32[128]{0:T(128)S(1)} %copy-done.65, f32[8192]{0:T(1024)S(1)} %copy-done.48, f32[8192]{0:T(1024)S(1)} %copy-done.27), kind=kOutput, calls=%fused_computation.182 | convolution fusion | flops 1619001344 | bytes 8553472 | tf_op jit(solution)/shard_map/transpose(jvp())/dot_general | solution.py:17
  714.7 8.2 fusion.217
  726.7 54.1 %while.52 = (s32[]{:T(128)}, f32[768,128]{1,0:T(8,128)}, s32[8,1024]{1,0:T(8,128)}, s32[]{:T(128)}, s32[8,1024]{1,0:T(8,128)}, /*index=5*/bf16[8,1024,128]{2,1,0:T(8,128)(2,1)S(1)}, s32[]{:T(128)}, s32[]{:T(128)}) while((s32[]{:T(128)}, f32[768,128]{1,0:T(8,128)}, s32[8,1024]{1,0:T(8,128)}, s32[]{:T(128)}, ...), condition=%wide.region_34.35_spmd.clone, body=%wide.region_33.34_spmd.clone.sunk | while | flops 215707648 | bytes 1099883 | solution.py:227
  733.5 6.1 fusion.265
  740.4 6.1 fusion.265
  747.3 6.1 fusion.265
  754.1 6.1 fusion.265
  761.0 6.1 fusion.265
  767.9 6.1 fusion.265
  774.8 6.1 fusion.265
  821.1 40.4 %all-reduce.20 = (f32[4]{0:T(128)S(1)}, f32[4]{0:T(128)S(1)}) all-reduce(f32[4]{0:T(128)S(1)} %pad_maximum_fusion.3, f32[4]{0:T(128)S(1)} %pad_maximum_fusion.4), channel_id=1, replica_groups=mesh['dp'=2,'region'=16] {'dp','region'}, use_global_device_ids=true, to_apply=%region_23.24 | all-reduce | flops 8 | bytes 64 | tf_op jit(solution)/shard_map/psum | solution.py:248
  (405 shorter events, 247.9 us)
Async XLA Ops:
  7.2 230.4 %all-reduce.26.cloned.1.call-start = ((), (), s32[]{:S(2)}) async-start(), calls=%async_computation.2 | async-start | bytes 8388608 | tf_op jit(solution)/shard_map/psum | solution.py:151
  66.6 171.0 %copy-start.23 = (s32[8192]{0:T(1024)S(1)}, s32[8192]{0:T(1024)}, u32[]{:S(2)}) copy-start(s32[8192]{0:T(1024)} %param.30) | copy-start | bytes 98308
  66.6 429.4 %reduce-scatter.5.cloned.1.call-start = ((), (), s32[]{:S(2)}) async-start(), calls=%async_computation.5 | async-start | bytes 589824 | tf_op jit(solution)/shard_map/reduce_scatter | solution.py:235
  72.1 174.1 %copy-start.64 = (f32[128]{0:T(128)}, f32[128]{0:T(128)S(1)}, u32[]{:S(2)}) copy-start(f32[128]{0:T(128)S(1)} %get-tuple-element.727) | copy-start | bytes 1540
  72.1 174.1 %copy-start.72 = (f32[128]{0:T(128)}, f32[128]{0:T(128)S(1)}, u32[]{:S(2)}) copy-start(f32[128]{0:T(128)S(1)} %get-tuple-element.726) | copy-start | bytes 1540
  72.2 192.6 %copy-start.66 = (f32[128]{0:T(128)}, f32[128]{0:T(128)S(1)}, u32[]{:S(2)}) copy-start(f32[128]{0:T(128)S(1)} %get-tuple-element.725) | copy-start | bytes 1540
  72.2 192.6 %copy-start.76 = (f32[128]{0:T(128)}, f32[128]{0:T(128)S(1)}, u32[]{:S(2)}) copy-start(f32[128]{0:T(128)S(1)} %get-tuple-element.724) | copy-start | bytes 1540
  72.2 211.5 %copy-start.68 = (f32[128]{0:T(128)}, f32[128]{0:T(128)S(1)}, u32[]{:S(2)}) copy-start(f32[128]{0:T(128)S(1)} %get-tuple-element.723) | copy-start | bytes 1540
  72.2 211.5 %copy-start.74 = (f32[128]{0:T(128)}, f32[128]{0:T(128)S(1)}, u32[]{:S(2)}) copy-start(f32[128]{0:T(128)S(1)} %get-tuple-element.722) | copy-start | bytes 1540
  72.2 218.8 %copy-start.60 = (f32[128]{0:T(128)}, f32[128]{0:T(128)S(1)}, u32[]{:S(2)}) copy-start(f32[128]{0:T(128)S(1)} %get-tuple-element.720) | copy-start | bytes 1540
  72.2 218.8 %copy-start.62 = (f32[128]{0:T(128)}, f32[128]{0:T(128)S(1)}, u32[]{:S(2)}) copy-start(f32[128]{0:T(128)S(1)} %get-tuple-element.721) | copy-start | bytes 1540
  445.4 183.5 %copy-start.25 = (f32[8192]{0:T(1024)S(1)}, f32[8192]{0:T(1024)}, u32[]{:S(2)}) copy-start(f32[8192]{0:T(1024)} %copy-done.24) | copy-start | bytes 98308
  445.4 183.5 %copy-start.61 = (f32[128]{0:T(128)S(1)}, f32[128]{0:T(128)}, u32[]{:S(2)}) copy-start(f32[128]{0:T(128)} %copy-done.60) | copy-start | bytes 1540
  445.4 183.5 %copy-start.63 = (f32[128]{0:T(128)S(1)}, f32[128]{0:T(128)}, u32[]{:S(2)}) copy-start(f32[128]{0:T(128)} %copy-done.62) | copy-start | bytes 1540
  446.1 182.8 %all-reduce.28.cloned.1.call-start = ((), (), s32[]{:S(2)}) async-start(), calls=%async_computation.3 | async-start | bytes 8388608 | tf_op jit(solution)/shard_map/psum | solution.py:203
  446.9 354.0 %all-reduce.30.cloned.1.call-start = ((), (), s32[]{:S(2)}) async-start(), calls=%async_computation.6 | async-start | bytes 303104 | tf_op jit(solution)/shard_map/psum | solution.py:210
  498.5 138.0 %copy-start.39 = (f32[8192]{0:T(1024)S(1)}, f32[8192]{0:T(1024)}, u32[]{:S(2)}) copy-start(f32[8192]{0:T(1024)} %copy-done.38) | copy-start | bytes 98308
  726.6 54.3 %copy-start.70 = (f32[128]{0:T(128)S(1)}, f32[128]{0:T(128)}, u32[]{:S(2)}) copy-start(f32[128]{0:T(128)} %get-tuple-element.582) | copy-start | bytes 1540
  726.6 54.3 %copy-start.71 = (f32[128]{0:T(128)S(1)}, f32[128]{0:T(128)}, u32[]{:S(2)}) copy-start(f32[128]{0:T(128)} %get-tuple-element.583) | copy-start | bytes 1540
  726.7 54.3 %copy-start.78 = (f32[128]{0:T(128)S(1)}, f32[128]{0:T(128)}, u32[]{:S(2)}) copy-start(f32[128]{0:T(128)} %get-tuple-element.585) | copy-start | bytes 1540
  726.7 54.2 %copy-start.79 = (f32[128]{0:T(128)S(1)}, f32[128]{0:T(128)}, u32[]{:S(2)}) copy-start(f32[128]{0:T(128)} %get-tuple-element.591) | copy-start | bytes 1540
  726.7 54.3 %copy-start.55 = (f32[128,128]{1,0:T(8,128)S(1)}, f32[128,128]{1,0:T(8,128)}, u32[]{:S(2)}) copy-start(f32[128,128]{1,0:T(8,128)} %fusion.109) | copy-start | bytes 196612
  726.7 61.6 %copy-start.45 = (f32[129,20]{0,1:T(8,128)S(1)}, f32[129,20]{0,1:T(8,128)}, u32[]{:S(2)}) copy-start(f32[129,20]{0,1:T(8,128)} %param.45) | copy-start | bytes 30964
  726.7 63.0 %copy-start.58 = (f32[1,768]{1,0:T(1,128)S(1)}, f32[1,768]{1,0:T(1,128)}, u32[]{:S(2)}) copy-start(f32[1,768]{1,0:T(1,128)} %param.39) | copy-start | bytes 9220
  780.8 88.5 %copy-start.13 = (f32[64,768]{1,0:T(8,128)S(1)}, f32[64,768]{1,0:T(8,128)}, u32[]{:S(2)}) copy-start(f32[64,768]{1,0:T(8,128)} %param.36) | copy-start | bytes 589828
  780.8 88.5 %copy-start.18 = (f32[64,768]{1,0:T(8,128)S(1)}, f32[64,768]{1,0:T(8,128)}, u32[]{:S(2)}) copy-start(f32[64,768]{1,0:T(8,128)} %get-tuple-element.693) | copy-start | bytes 589828
  780.9 88.5 %copy-start.19 = (f32[64,768]{1,0:T(8,128)S(1)}, f32[64,768]{1,0:T(8,128)}, u32[]{:S(2)}) copy-start(f32[64,768]{1,0:T(8,128)} %get-tuple-element.694) | copy-start | bytes 589828
  783.8 28.3 %reduce-scatter.3.cloned.1.call-start = ((), (), s32[]{:S(2)}) async-start(), calls=%async_computation.4 | async-start | bytes 589824 | tf_op jit(solution)/shard_map/reduce_scatter | solution.py:234
  789.8 81.2 %copy-start.53 = (f32[129,20]{0,1:T(8,128)}, f32[129,20]{0,1:T(8,128)S(1)}, u32[]{:S(2)}) copy-start(f32[129,20]{0,1:T(8,128)S(1)} %get-tuple-element.674) | copy-start | bytes 30964
  789.8 81.2 %copy-start.54 = (f32[129,20]{0,1:T(8,128)}, f32[129,20]{0,1:T(8,128)S(1)}, u32[]{:S(2)}) copy-start(f32[129,20]{0,1:T(8,128)S(1)} %get-tuple-element.675) | copy-start | bytes 30964
  813.9 57.1 %copy-start.20 = (f32[768,64]{0,1:T(8,128)}, f32[768,64]{0,1:T(8,128)S(1)}, u32[]{:S(2)}) copy-start(f32[768,64]{0,1:T(8,128)S(1)} %get-tuple-element.687) | copy-start | bytes 589828
  813.9 57.1 %copy-start.21 = (f32[768,64]{0,1:T(8,128)}, f32[768,64]{0,1:T(8,128)S(1)}, u32[]{:S(2)}) copy-start(f32[768,64]{0,1:T(8,128)S(1)} %get-tuple-element.688) | copy-start | bytes 589828
  (56 other events, 700.6 us)
Sparse Core Ops, SparseCore 0:
  66.8 170.7 all-reduce.25
  446.3 6.7 reduce-scatter.4
  458.7 170.1 all-reduce.27
  783.9 16.9 all-reduce.29
  803.1 9.0 reduce-scatter.2
where the time goes:
time: 888 us; the launch traced here: 878 us
  waiting for transfers between devices  301 us (34%)
  matrix products  299 us (34%)
  other arithmetic  96.1 us (11%)
  blocking collectives  93.8 us (11%)
  local copies, waits for them, and re-layouts  50 us (6%)
  between operations  31.2 us (4%)
    psum x1, waiting for transfers between devices, on_device(): enc_total = lax.psum(partial_pre, 'region')  165 us
    psum x1, waiting for transfers between devices, on_device(): hidden_grad, recon_region = lax.psum((back_hidden, recon_sum), 'region')  130 us
    dot_general x15, matrix products, matmul(): jnp.dot(left, right, precision=highest, preferred_element_type=jnp.float32)  97.3 us
    dot_general x8, matrix products, decode_block(): jnp.dot(hidden_low, dec_low, preferred_element_type=jnp.float32)  87 us
    dot_general x8, matrix products, encode_back(): lax.dot_general(mask_rows, inputs[2], (((0,), (0,)), ((), ())), preferred...  47.4 us
    dot_general x8, matrix products, encode_block(): jnp.dot(mask_rows, enc_low, preferred_element_type=jnp.float32)  44.5 us
    psum x1, blocking collectives, on_device(): hidden_grad, recon_region = lax.psum((back_hidden, recon_sum), 'region')  43.1 us
    psum x1, blocking collectives, on_device(): lax.psum((weight_squares(enc_weight, dec_weight, region_vecs, slot_rows),...  40.4 us
  transfers between devices with their start and end apart: 5, of which 4 were waited for; matrix products, arithmetic and copies ran while one was open for 2% of the time, Pallas kernels for 0%

commit v1 on v0

--- a/solution.py
+++ b/solution.py
@@ -148,7 +148,11 @@
         jnp.float32
     )
     onehot_low = onehot.astype(jnp.bfloat16)
-    enc_total = lax.psum(partial_pre, "region")
+    enc_total = partial_pre
+    for hop in (1, 2, 4, 8):
+        enc_total = enc_total + lax.ppermute(
+            enc_total, "region", [(dev, dev ^ hop) for dev in range(16)]
+        )
     pre_one = enc_total + matmul(onehot, trunk_rows[:BATCHES])
     (decoded, diverge), pull_back = jax.vjp(
         lambda pre_in, weights, head_part: trunk_forward(

time: 888 us -> 1170 us (1.32)
  waiting for transfers between devices: 301 us -> 568 us
    ppermute x0 -> x4, waiting for transfers between devices: none -> 441 us  [on_device(): lax.ppermute(enc_total, 'region', [(dev, dev ^ hop) for dev in range(16)])]
    psum x1 -> x0, waiting for transfers between devices: 165 us -> none  [on_device(): enc_total = lax.psum(partial_pre, 'region')]
    reduce_sum x4 -> x5, other arithmetic: 23.7 us -> 28.7 us  [layer_norm(): centre = values - jnp.mean(values, axis=-1, keepdims=True)]
  transfers between devices with their start and end apart: 5 -> 8, of which waited for: 4 -> 7; matrix products, arithmetic and copies ran while one was open for 2% -> 2% of each run, Pallas kernels for 0% -> 0%
where the time goes in v1:
time: 1170 us; the launch traced here: 1160 us
  waiting for transfers between devices  568 us (49%)
  matrix products  297 us (25%)
  other arithmetic  107 us (9%)
  blocking collectives  96.1 us (8%)
  local copies, waits for them, and re-layouts  49.2 us (4%)
  between operations  32.6 us (3%)
    ppermute x4, waiting for transfers between devices, on_device(): lax.ppermute(enc_total, 'region', [(dev, dev ^ hop) for dev in range(16)])  441 us
    psum x1, waiting for transfers between devices, on_device(): hidden_grad, recon_region = lax.psum((back_hidden, recon_sum), 'region')  120 us
    dot_general x15, matrix products, matmul(): jnp.dot(left, right, precision=highest, preferred_element_type=jnp.float32)  94.6 us
    dot_general x8, matrix products, decode_block(): jnp.dot(hidden_low, dec_low, preferred_element_type=jnp.float32)  87 us
    dot_general x8, matrix products, encode_back(): lax.dot_general(mask_rows, inputs[2], (((0,), (0,)), ((), ())), preferred...  47.4 us
    psum x1, blocking collectives, on_device(): hidden_grad, recon_region = lax.psum((back_hidden, recon_sum), 'region')  45.1 us
    dot_general x8, matrix products, encode_block(): jnp.dot(mask_rows, enc_low, preferred_element_type=jnp.float32)  44.5 us
    psum x1, blocking collectives, on_device(): lax.psum((weight_squares(enc_weight, dec_weight, region_vecs, slot_rows),...  40.5 us
  transfers between devices with their start and end apart: 8, of which 7 were waited for; matrix products, arithmetic and copies ran while one was open for 2% of the time, Pallas kernels for 0%

profile of v1, /device:TPU:0, one launch (start us, length us, event | category | flops | bytes accessed | tf_op | source)
XLA Modules:
  0.0 1163.4 jit_solution(13957853852231010259)
XLA Ops:
  16.3 51.1 %while.50 = (s32[]{:T(128)}, f32[8,1024,128]{2,1,0:T(8,128)}, s32[8,1024]{1,0:T(8,128)}, s32[]{:T(128)}, s32[8,1024]{1,0:T(8,128)}, /*index=5*/bf16[768,128]{1,0:T(8,128)(2,1)S(1)}, s32[]{:T(128)}) while((s32[]{:T(128)}, f32[8,1024,128]{2,1,0:T(8,128)}, s32[8,1024]{1,0:T(8,128)}, s32[]{:T(128)}, s32[8,1024]{1,0:T(8,128)}, ...), condition=%wide.region_1.2_spmd, body=%wide.region_0.1_spmd.sunk | while | flops 215511040 | bytes 770645 | solution.py:143
  70.2 91.1 %collective-permute-done = f32[8192,128]{1,0:T(8,128)S(1)} collective-permute-done((f32[8192,128]{1,0:T(8,128)}, f32[8192,128]{1,0:T(8,128)S(1)}, u32[]{:S(2)}, u32[]{:S(2)}) %collective-permute-start) | collective-permute-done | bytes 4194336 | tf_op jit(solution)/shard_map/ppermute | solution.py:153
  165.9 90.3 %collective-permute-done.1 = f32[8192,128]{1,0:T(8,128)S(1)} collective-permute-done((f32[8192,128]{1,0:T(8,128)S(1)}, f32[8192,128]{1,0:T(8,128)S(1)}, u32[]{:S(2)}, u32[]{:S(2)}) %collective-permute-start.1) | collective-permute-done | bytes 4194336 | tf_op jit(solution)/shard_map/ppermute | solution.py:153
  258.3 89.7 %collective-permute-done.2 = f32[8192,128]{1,0:T(8,128)S(1)} collective-permute-done((f32[8192,128]{1,0:T(8,128)S(1)}, f32[8192,128]{1,0:T(8,128)S(1)}, u32[]{:S(2)}, u32[]{:S(2)}) %collective-permute-start.2) | collective-permute-done | bytes 4194336 | tf_op jit(solution)/shard_map/ppermute | solution.py:153
  361.6 170.2 %collective-permute-done.3 = f32[8192,128]{1,0:T(8,128)} collective-permute-done((f32[8192,128]{1,0:T(8,128)}, f32[8192,128]{1,0:T(8,128)}, u32[]{:S(2)}, u32[]{:S(2)}) %collective-permute-start.3) | collective-permute-done | bytes 4194336 | tf_op jit(solution)/shard_map/ppermute | solution.py:153
  539.2 8.2 fusion.227
  562.9 6.7 fusion.189
  592.3 146.1 %while.51 = (s32[]{:T(128)}, f32[128,768]{1,0:T(8,128)S(1)}, f32[768]{0:T(1024)S(1)}, f32[768]{0:T(1024)}, f32[]{:T(128)}, /*index=5*/f32[8,1024,128]{2,1,0:T(8,...) while((s32[]{:T(128)}, f32[128,768]{1,0:T(8,128)S(1)}, ...), condition=%wide.region_14.15_spmd.clone, body=%wide.region_10.14_spmd.clone.sunk | while | flops 643528960 | bytes 19630788 | solution.py:203
  594.1 10.9 fusion.262
  612.3 10.9 fusion.262
  630.5 10.9 fusion.262
  648.8 10.9 fusion.262
  667.0 10.9 fusion.262
  685.3 10.9 fusion.262
  703.5 10.9 fusion.262
  721.7 10.9 fusion.262
  745.8 45.1 %psum.56 = f32[]{:T(128)} all-reduce(f32[]{:T(128)} %get-tuple-element.495), channel_id=1, replica_groups=mesh['dp'=2,'region'=16] {'region'}, use_global_device_ids=true, to_apply=%region_15.16 | all-reduce | flops 1 | bytes 8 | tf_op jit(solution)/shard_map/psum | solution.py:207
  793.3 120.4 %all-reduce.25.cloned.1.call-done = f32[8192,128]{1,0:T(8,128)} async-done(((f32[8192,128]{1,0:T(8,128)}), f32[8192,128]{1,0:T(8,128)}) %all-reduce.25.cloned.1.call-update) | async-done | bytes 4194320 | tf_op jit(solution)/shard_map/psum | solution.py:207
  913.8 7.6 fusion.210
  926.7 6.4 multiply_reduce_fusion.2
  947.6 11.2 multiply_reduce_fusion.1
  958.8 11.3 fusion.109
  980.5 8.0 multiply_reduce_fusion
  988.5 10.9 fusion.103
  999.5 8.2 fusion.219
  1011.6 54.1 %while.52 = (s32[]{:T(128)}, f32[768,128]{1,0:T(8,128)}, s32[8,1024]{1,0:T(8,128)}, s32[]{:T(128)}, s32[8,1024]{1,0:T(8,128)}, /*index=5*/bf16[8,1024,128]{2,1,0:T(8,128)(2,1)S(1)}, s32[]{:T(128)}, s32[]{:T(128)}) while((s32[]{:T(128)}, f32[768,128]{1,0:T(8,128)}, s32[8,1024]{1,0:T(8,128)}, s32[]{:T(128)}, ...), condition=%wide.region_33.34_spmd.clone, body=%wide.region_32.33_spmd.clone.sunk | while | flops 215707648 | bytes 1099883 | solution.py:231
  1018.3 6.1 fusion.267
  1025.2 6.1 fusion.267
  1032.1 6.1 fusion.267
  1039.0 6.1 fusion.267
  1045.8 6.1 fusion.267
  1106.1 40.5 %all-reduce.20 = (f32[4]{0:T(128)S(1)}, f32[4]{0:T(128)S(1)}) all-reduce(f32[4]{0:T(128)S(1)} %pad_maximum_fusion.3, f32[4]{0:T(128)S(1)} %pad_maximum_fusion.4), channel_id=1, replica_groups=mesh['dp'=2,'region'=16] {'dp','region'}, use_global_device_ids=true, to_apply=%region_22.23 | all-reduce | flops 8 | bytes 64 | tf_op jit(solution)/shard_map/psum | solution.py:252
  (414 shorter events, 281.7 us)
Async XLA Ops:
  8.0 782.9 %reduce-scatter.5.cloned.1.call-start = ((), (), s32[]{:S(2)}) async-start(), calls=%async_computation.4 | async-start | bytes 589824 | tf_op jit(solution)/shard_map/reduce_scatter | solution.py:239
  67.4 93.9 %collective-permute-start = (f32[8192,128]{1,0:T(8,128)}, f32[8192,128]{1,0:T(8,128)S(1)}, u32[]{:S(2)}, u32[]{:S(2)}) collective-permute-start(f32[8192,128]{1,0:T(8,128)} %bitcast.124), channel_id=1, source_target_pairs={{0,1},{1,0},{2,3},{3,2},{4,5},{5,4},{6,7},{7,6},{8,9},{9,8},{10,11... | collective-permute-start | bytes 12582920 | tf_op jit(solution)/shard_map/ppermute | solution.py:153
  164.0 92.2 %collective-permute-start.1 = (f32[8192,128]{1,0:T(8,128)S(1)}, f32[8192,128]{1,0:T(8,128)S(1)}, u32[]{:S(2)}, u32[]{:S(2)}) collective-permute-start(f32[8192,128]{1,0:T(8,128)S(1)} %bitcast_add_fusion), channel_id=1, source_target_pairs={{0,2},{1,3},{2,0},{3,1},{4,6},{5,7},{6,4},{7,5},{8,10},{9,11},{10,... | collective-permute-start | bytes 12582920 | tf_op jit(solution)/shard_map/ppermute | solution.py:153
  256.6 95.9 %copy-start.11 = (f32[64,768]{1,0:T(8,128)S(1)}, f32[64,768]{1,0:T(8,128)}, u32[]{:S(2)}) copy-start(f32[64,768]{1,0:T(8,128)} %param.36) | copy-start | bytes 589828
  256.7 95.9 %copy-start.56 = (f32[8192]{0:T(1024)S(1)}, f32[8192]{0:T(1024)}, u32[]{:S(2)}) copy-start(f32[8192]{0:T(1024)} %param.32) | copy-start | bytes 98308
  256.7 96.5 %copy-start.57 = (f32[1,768]{1,0:T(1,128)S(1)}, f32[1,768]{1,0:T(1,128)}, u32[]{:S(2)}) copy-start(f32[1,768]{1,0:T(1,128)} %param.39) | copy-start | bytes 9220
  256.7 100.5 %copy-start.43 = (f32[129,20]{0,1:T(8,128)S(1)}, f32[129,20]{0,1:T(8,128)}, u32[]{:S(2)}) copy-start(f32[129,20]{0,1:T(8,128)} %param.45) | copy-start | bytes 30964
  256.7 100.7 %copy-start.15 = (f32[290,128]{1,0:T(8,128)S(1)}, f32[290,128]{1,0:T(8,128)}, u32[]{:S(2)}) copy-start(f32[290,128]{1,0:T(8,128)} %param.42) | copy-start | bytes 445444
  256.7 101.4 %copy-start.23 = (s32[8192]{0:T(1024)S(1)}, s32[8192]{0:T(1024)}, u32[]{:S(2)}) copy-start(s32[8192]{0:T(1024)} %param.30) | copy-start | bytes 98308
  256.7 91.3 %collective-permute-start.2 = (f32[8192,128]{1,0:T(8,128)S(1)}, f32[8192,128]{1,0:T(8,128)S(1)}, u32[]{:S(2)}, u32[]{:S(2)}) collective-permute-start(f32[8192,128]{1,0:T(8,128)S(1)} %add.711), channel_id=1, source_target_pairs={{0,4},{1,5},{2,6},{3,7},{4,0},{5,1},{6,2},{7,3},{8,12},{9,13},{10,... | collective-permute-start | bytes 12582920 | tf_op jit(solution)/shard_map/ppermute | solution.py:153
  350.4 181.4 %collective-permute-start.3 = (f32[8192,128]{1,0:T(8,128)}, f32[8192,128]{1,0:T(8,128)}, u32[]{:S(2)}, u32[]{:S(2)}) collective-permute-start(f32[8192,128]{1,0:T(8,128)} %add.712), channel_id=1, source_target_pairs={{0,8},{1,9},{2,10},{3,11},{4,12},{5,13},{6,14},{7,15},{8,0},{9,1},... | collective-permute-start | bytes 12582920 | tf_op jit(solution)/shard_map/ppermute | solution.py:153
  357.4 181.7 %copy-start.64 = (f32[128]{0:T(128)}, f32[128]{0:T(128)S(1)}, u32[]{:S(2)}) copy-start(f32[128]{0:T(128)S(1)} %get-tuple-element.729) | copy-start | bytes 1540
  357.4 181.7 %copy-start.72 = (f32[128]{0:T(128)}, f32[128]{0:T(128)S(1)}, u32[]{:S(2)}) copy-start(f32[128]{0:T(128)S(1)} %get-tuple-element.728) | copy-start | bytes 1540
  357.4 200.3 %copy-start.66 = (f32[128]{0:T(128)}, f32[128]{0:T(128)S(1)}, u32[]{:S(2)}) copy-start(f32[128]{0:T(128)S(1)} %get-tuple-element.727) | copy-start | bytes 1540
  357.4 200.3 %copy-start.76 = (f32[128]{0:T(128)}, f32[128]{0:T(128)S(1)}, u32[]{:S(2)}) copy-start(f32[128]{0:T(128)S(1)} %get-tuple-element.726) | copy-start | bytes 1540
  357.5 219.2 %copy-start.68 = (f32[128]{0:T(128)}, f32[128]{0:T(128)S(1)}, u32[]{:S(2)}) copy-start(f32[128]{0:T(128)S(1)} %get-tuple-element.725) | copy-start | bytes 1540
  357.5 219.2 %copy-start.74 = (f32[128]{0:T(128)}, f32[128]{0:T(128)S(1)}, u32[]{:S(2)}) copy-start(f32[128]{0:T(128)S(1)} %get-tuple-element.724) | copy-start | bytes 1540
  357.5 226.5 %copy-start.60 = (f32[128]{0:T(128)}, f32[128]{0:T(128)S(1)}, u32[]{:S(2)}) copy-start(f32[128]{0:T(128)S(1)} %get-tuple-element.722) | copy-start | bytes 1540
  357.5 226.5 %copy-start.62 = (f32[128]{0:T(128)}, f32[128]{0:T(128)S(1)}, u32[]{:S(2)}) copy-start(f32[128]{0:T(128)S(1)} %get-tuple-element.723) | copy-start | bytes 1540
  738.4 175.3 %copy-start.25 = (f32[8192]{0:T(1024)S(1)}, f32[8192]{0:T(1024)}, u32[]{:S(2)}) copy-start(f32[8192]{0:T(1024)} %copy-done.24) | copy-start | bytes 98308
  738.4 175.3 %copy-start.61 = (f32[128]{0:T(128)S(1)}, f32[128]{0:T(128)}, u32[]{:S(2)}) copy-start(f32[128]{0:T(128)} %copy-done.60) | copy-start | bytes 1540
  738.5 175.3 %copy-start.63 = (f32[128]{0:T(128)S(1)}, f32[128]{0:T(128)}, u32[]{:S(2)}) copy-start(f32[128]{0:T(128)} %copy-done.62) | copy-start | bytes 1540
  739.1 174.6 %all-reduce.25.cloned.1.call-start = ((), (), s32[]{:S(2)}) async-start(), calls=%async_computation.2 | async-start | bytes 8388608 | tf_op jit(solution)/shard_map/psum | solution.py:207
  739.7 346.1 %all-reduce.27.cloned.1.call-start = ((), (), s32[]{:S(2)}) async-start(), calls=%async_computation.5 | async-start | bytes 303104 | tf_op jit(solution)/shard_map/psum | solution.py:214
  793.3 128.0 %copy-start.39 = (f32[8192]{0:T(1024)S(1)}, f32[8192]{0:T(1024)}, u32[]{:S(2)}) copy-start(f32[8192]{0:T(1024)} %copy-done.38) | copy-start | bytes 98308
  1011.6 63.0 %copy-start.58 = (f32[1,768]{1,0:T(1,128)S(1)}, f32[1,768]{1,0:T(1,128)}, u32[]{:S(2)}) copy-start(f32[1,768]{1,0:T(1,128)} %param.39) | copy-start | bytes 9220
  1065.7 88.7 %copy-start.13 = (f32[64,768]{1,0:T(8,128)S(1)}, f32[64,768]{1,0:T(8,128)}, u32[]{:S(2)}) copy-start(f32[64,768]{1,0:T(8,128)} %param.36) | copy-start | bytes 589828
  1065.7 88.7 %copy-start.18 = (f32[64,768]{1,0:T(8,128)S(1)}, f32[64,768]{1,0:T(8,128)}, u32[]{:S(2)}) copy-start(f32[64,768]{1,0:T(8,128)} %get-tuple-element.693) | copy-start | bytes 589828
  1065.7 88.7 %copy-start.19 = (f32[64,768]{1,0:T(8,128)S(1)}, f32[64,768]{1,0:T(8,128)}, u32[]{:S(2)}) copy-start(f32[64,768]{1,0:T(8,128)} %get-tuple-element.694) | copy-start | bytes 589828
  1068.6 28.4 %reduce-scatter.3.cloned.1.call-start = ((), (), s32[]{:S(2)}) async-start(), calls=%async_computation.3 | async-start | bytes 589824 | tf_op jit(solution)/shard_map/reduce_scatter | solution.py:238
  1074.6 81.4 %copy-start.53 = (f32[129,20]{0,1:T(8,128)}, f32[129,20]{0,1:T(8,128)S(1)}, u32[]{:S(2)}) copy-start(f32[129,20]{0,1:T(8,128)S(1)} %get-tuple-element.674) | copy-start | bytes 30964
  1074.6 81.4 %copy-start.54 = (f32[129,20]{0,1:T(8,128)}, f32[129,20]{0,1:T(8,128)S(1)}, u32[]{:S(2)}) copy-start(f32[129,20]{0,1:T(8,128)S(1)} %get-tuple-element.675) | copy-start | bytes 30964
  (59 other events, 1140.9 us)
Sparse Core Ops, SparseCore 0:
  739.3 8.1 reduce-scatter.4
  1068.8 16.9 all-reduce.26
  1088.0 8.9 reduce-scatter.2
Sparse Core Ops, SparseCore 1:
  745.3 168.4 all-reduce.24
